TPU v7x, 32 devices: a whole 2x2x4 slice. The times are simulated.
32 devices in a mesh: tm: 4 (over y, core), chan: 8 (over z, x).
Axes of the slice: x: 2, y: 2, z: 4, core: 2. Of those that a mesh axis runs over, the one named last changes fastest.
Arguments:
- voltages: bfloat16 [1024, 274432], P('chan', 'tm'), may hold values from -6 to 6
- taper_weights: float32 [4, 1024], replicated, may hold values from -1 to 1
Outputs:
- visibilities: bfloat16 [256, 2, 1024, 1024], P(('tm', 'chan'))
All inputs are finite; a program needn't handle non-finite values.
Results may differ from a plain program's by a relative error of at most 0.0071.
Values may be sent and summed in bfloat16 or wider, within the bound.
A program may use at most 192 MiB of HBM per device.

v0:
```python
import math

import jax
import jax.numpy as jnp
from jax import lax
from jax.sharding import PartitionSpec as P

L = 1024
CH = 256
TAPS = 4
SPEC_DEV = 64


def dft_table(length, channels):
    sample_idx = jnp.arange(length, dtype=jnp.int32)[:, None]
    column = jnp.arange(2 * channels, dtype=jnp.int32)[None, :]
    freq = column // 2 + channels // 2
    phase = (sample_idx * freq % length).astype(jnp.float32) * (2.0 * math.pi / length)
    values = jnp.where(column % 2 == 0, jnp.cos(phase), -jnp.sin(phase))
    return values.astype(jnp.bfloat16)


def contract(rows, cols):
    return lax.dot_general(rows, cols, (((1,), (1,)), ((), ())), preferred_element_type=jnp.float32)


def correlate(spec):
    real_part = spec[0]
    imag_part = spec[1]
    left_rows = jnp.concatenate([real_part, imag_part], axis=1)
    other_rows = jnp.concatenate([imag_part, -real_part], axis=1)
    count = left_rows.shape[0]
    stacked = jnp.concatenate([left_rows, other_rows], axis=0)
    return contract(stacked, left_rows).reshape(2, count, count)


def shards(voltages, taper_weights):
    time_count = lax.axis_size("tm")
    chan_count = lax.axis_size("chan")
    inputs_here = voltages.shape[0]
    frame_count = SPEC_DEV + TAPS - 1
    frames = voltages.reshape(inputs_here, frame_count, L)
    filtered = taper_weights[0][None, None, :] * frames[:, 0:SPEC_DEV, :].astype(jnp.float32)
    for tap_index in range(1, TAPS):
        filtered = filtered + taper_weights[tap_index][None, None, :] * frames[
            :, tap_index : tap_index + SPEC_DEV, :
        ].astype(jnp.float32)
    filtered = filtered.astype(jnp.bfloat16)
    table = dft_table(L, CH)
    spectra = jnp.einsum(
        "isn,nc->cis", filtered, table, preferred_element_type=jnp.float32
    ) * L ** (-0.5)
    spectra = spectra.astype(jnp.bfloat16)
    per_owner = CH // (time_count * chan_count)
    spectra = spectra.reshape(time_count, chan_count, per_owner, 2, inputs_here, SPEC_DEV)
    scale = 1.0 / (SPEC_DEV * time_count)
    turned = lax.all_to_all(spectra, "tm", split_axis=0, concat_axis=5, tiled=True)
    piece = lax.all_to_all(turned, "chan", split_axis=1, concat_axis=4, tiled=True)
    flat = piece.reshape(piece.shape[2], 2, piece.shape[4], piece.shape[5])
    visibilities = lax.map(correlate, flat) * scale
    return visibilities.astype(jnp.bfloat16)


def solution(mesh):
    placed = (P("chan", "tm"), P())
    return jax.shard_map(
        shards,
        mesh=mesh,
        in_specs=placed,
        out_specs=P(("tm", "chan"), None, None, None),
        check_vma=False,
    )
```

profile of v0, /device:TPU:1, one launch (start us, length us, event | category | flops | bytes accessed | tf_op | source)
XLA Modules:
  0.0 490.0 jit_solution(273203004446831901)
XLA Ops:
  0.0 0.9 fusion.39
  0.9 23.5 %copy.14 = bf16[128,68608]{0,1:T(8,128)(2,1)} copy(bf16[128,68608]{1,0:T(8,128)(2,1)} %param.4) | data formatting | bytes 35127296 | tf_op args[0]
  24.4 9.2 %fusion.43 = bf16[1024,512,1]{0,1,2:T(8,128)(2,1)S(1)} fusion(s32[512]{0:T(512)S(1)} %fusion.29, pred[512]{0:T(512)(128)(4,1)S(1)} %fusion.27), kind=kLoop, calls=%fused_computation.29.clone.clone.2 | loop fusion | flops 8912896 | bytes 1051136 | tf_op jit(solution)/shard_map/isn,nc->cis/dot_general | solution.py:50
  33.6 28.2 %multiply_convert_fusion.1 = bf16[512,128,64]{1,0,2:T(8,128)(2,1)} fusion(bf16[128,67,1024]{0,2,1:T(8,128)(2,1)} %bitcast.39, f32[1024]{0:T(1024)S(1)} %bitcast.43, f32[1024]{0:T(1024)S(1)} %bitcast.44, f32[1024]{0:T(1024)S(1)} %bitcast.42, f32[1024]{0:T(1024)S(1)} %bitcast.41, bf16[1024,512,1]{0,1,2:T(8,128)(2,1)S(1)} %fusion.43), kind=kOutput, calls=%fused_computation.17 | convolution fusion | flops 8698986496 | bytes 76562432 | tf_op jit(solution)/shard_map/isn,nc->cis/dot_general | solution.py:50
  61.8 16.5 %copy.16 = bf16[4,8,8,2,128,64]{4,5,3,2,1,0:T(8,128)(2,1)} copy(bf16[4,8,8,2,128,64]{4,3,2,1,0,5:T(2,128)(2,1)} %bitcast.40) | data formatting | bytes 16777216 | tf_op jit(solution)/shard_map/reshape | solution.py:55
  78.3 100.5 %all_to_all.33 = bf16[4,8,8,2,128,64]{4,5,3,2,1,0:T(8,128)(2,1)} all-to-all(bf16[4,8,8,2,128,64]{4,5,3,2,1,0:T(8,128)(2,1)} %copy.16), channel_id=1, replica_groups=mesh['tm'=4,'chan'=8] {'tm'}, dimensions={0} | all-to-all | bytes 16777216 | tf_op jit(solution)/shard_map/all_to_all | solution.py:57
  178.8 9.8 %copy.17 = bf16[4,8,8,2,128,64]{4,5,0,3,2,1:T(8,128)(2,1)} copy(bf16[4,8,8,2,128,64]{4,5,3,2,1,0:T(8,128)(2,1)} %all_to_all.33) | data formatting | bytes 16777216 | tf_op jit(solution)/shard_map/all_to_all | solution.py:57
  188.5 6.1 %all-to-all-start.1 = ((bf16[1,8,8,2,128,256]{4,5,3,2,0,1:T(8,128)(2,1)}), bf16[1,8,8,2,128,256]{4,5,3,2,0,1:T(8,128)(2,1)}, u32[]{:S(2)}, u32[]{:S(2)}) async-start(bf16[1,8,8,2,128,256]{4,5,3,2,0,1:T(8,128)(2,1)} %bitcast.37), calls=%async_computation.1 | async-start | bytes 16777216 | tf_op jit(solution)/shard_map/all_to_all | solution.py:58
  194.7 181.9 %all-to-all-done.1 = bf16[1,8,8,2,128,256]{4,5,3,2,0,1:T(8,128)(2,1)} async-done(((bf16[1,8,8,2,128,256]{4,5,3,2,0,1:T(8,128)(2,1)}), bf16[1,8,8,2,128,256]{4,5,3,2,0,1:T(8,128)(2,1)}, u32[]{:S(2)}, u32[]{:S(2)}) %all-to-all-start.1) | async-done | bytes 8388640 | tf_op jit(solution)/shard_map/all_to_all | solution.py:58
  376.6 11.4 %copy.19 = bf16[1,8,8,2,128,256]{5,4,1,3,2,0:T(8,128)(2,1)} copy(bf16[1,8,8,2,128,256]{4,5,3,2,0,1:T(8,128)(2,1)} %all-to-all-done.1) | data formatting | bytes 16777216 | tf_op jit(solution)/shard_map/all_to_all | solution.py:58
  387.9 69.3 %while.10 = (s32[]{:T(128)}, f32[8,2,1024,1024]{3,2,1,0:T(8,128)}, bf16[8,2,1024,256]{3,2,1,0:T(8,128)(2,1)}, s32[]{:T(128)}, s32[]{:T(128)}, /*index=5*/s32[]{}) while((s32[]{:T(128)}, f32[8,2,1024,1024]{3,2,1,0:T(8,128)}, bf16[8,2,1024,256]{3,2,1,0:T(8,128)(2,1)}, s32[]{:T(128)}, s32[]{:T(128)}, /*index=5*/s32[]{}) %tuple.27), condition=%wide.region_1.2_spmd, body=%wide.region_0.1_spmd.sunk | while | flops 2158231552 | bytes 29360732 | solution.py:60
  387.9 1.1 fusion.51
  389.1 1.1 dynamic-slice_bitcast_fusion.4
  390.1 2.4 fusion.52
  392.5 4.1 constant_dynamic-update-slice_fusion.2
  396.6 1.1 fusion.51
  397.7 1.1 dynamic-slice_bitcast_fusion.4
  398.8 2.4 fusion.52
  401.2 4.1 constant_dynamic-update-slice_fusion.2
  405.3 1.1 fusion.51
  406.4 1.1 dynamic-slice_bitcast_fusion.4
  407.5 2.4 fusion.52
  409.9 4.1 constant_dynamic-update-slice_fusion.2
  413.9 1.1 fusion.51
  415.1 1.1 dynamic-slice_bitcast_fusion.4
  416.1 2.4 fusion.52
  418.5 4.1 constant_dynamic-update-slice_fusion.2
  422.6 1.1 fusion.51
  423.7 1.1 dynamic-slice_bitcast_fusion.4
  424.8 2.4 fusion.52
  427.2 4.1 constant_dynamic-update-slice_fusion.2
  431.3 1.1 fusion.51
  432.4 1.1 dynamic-slice_bitcast_fusion.4
  433.5 2.4 fusion.52
  435.9 4.1 constant_dynamic-update-slice_fusion.2
  439.9 1.1 fusion.51
  441.0 1.1 dynamic-slice_bitcast_fusion.4
  442.1 2.4 fusion.52
  444.6 4.1 constant_dynamic-update-slice_fusion.2
  448.6 1.1 fusion.51
  449.7 1.1 dynamic-slice_bitcast_fusion.4
  450.8 2.4 fusion.52
  453.2 4.1 constant_dynamic-update-slice_fusion.2
  457.3 32.7 %multiply_convert_fusion = bf16[8,2,1024,1024]{3,2,1,0:T(8,128)(2,1)} fusion(f32[8,2,1024,1024]{3,2,1,0:T(8,128)} %get-tuple-element.22), kind=kLoop, calls=%fused_computation.15 | loop fusion | flops 33554432 | bytes 100663296 | tf_op jit(solution)/shard_map/convert_element_type | solution.py:61
  (3 shorter events, 0.0 us)
Async XLA Ops:
  188.5 188.0 %all-to-all-start.1 = ((bf16[1,8,8,2,128,256]{4,5,3,2,0,1:T(8,128)(2,1)}), bf16[1,8,8,2,128,256]{4,5,3,2,0,1:T(8,128)(2,1)}, u32[]{:S(2)}, u32[]{:S(2)}) async-start(bf16[1,8,8,2,128,256]{4,5,3,2,0,1:T(8,128)(2,1)} %bitcast.37), calls=%async_computation.1 | async-start | bytes 16777216 | tf_op jit(solution)/shard_map/all_to_all | solution.py:58
where the time goes:
time: 494 us; the launch traced here: 490 us
  waiting for transfers between devices  182 us (37%)
  local copies, waits for them, and re-layouts  103 us (21%)
  blocking collectives  100 us (20%)
  other arithmetic  50.7 us (10%)
  matrix products  47.4 us (10%)
  starting transfers between devices  6.12 us (1%)
    all_to_all x1, waiting for transfers between devices, shards(): lax.all_to_all(turned, 'chan', split_axis=1, concat_axis=4, tiled=True)  182 us
    all_to_all x1, blocking collectives, shards(): lax.all_to_all(spectra, 'tm', split_axis=0, concat_axis=5, tiled=True)  100 us
    convert_element_type x1, other arithmetic, shards(): return visibilities.astype(jnp.bfloat16)  32.7 us
    dynamic_update_slice x8, local copies, waits for them, and re-layouts, shards(): visibilities = lax.map(correlate, flat) * scale  32.5 us
    dot_general x1, matrix products, shards(): jnp.einsum('isn,nc->cis', filtered, table, preferred_element_type=jnp.flo...  28.2 us
    unnamed x1, local copies, waits for them, and re-layouts  23.5 us
    dot_general x8, matrix products, contract(): lax.dot_general(rows, cols, (((1,), (1,)), ((), ())), preferred_element_t...  19.2 us
    reshape x1, local copies, waits for them, and re-layouts, shards(): spectra.reshape(time_count, chan_count, per_owner, 2, inputs_here, SPEC_DEV)  16.5 us
  transfers between devices with their start and end apart: 1, of which 1 were waited for; matrix products, arithmetic and copies ran while one was open for 0% of the time, Pallas kernels for 0%

commit v1 on v0

--- a/solution.py
+++ b/solution.py
@@ -1,14 +1,242 @@
+import functools
 import math
 
 import jax
 import jax.numpy as jnp
+import numpy as np
 from jax import lax
+from jax.experimental import pallas as pl
+from jax.experimental.pallas import tpu as pltpu
 from jax.sharding import PartitionSpec as P
 
 L = 1024
 CH = 256
 TAPS = 4
 SPEC_DEV = 64
+MIB = 1024 * 1024
+MESH = pl.DeviceIdType.MESH
+
+STEP = 16
+GROUP = 4
+
+
+def table_rows():
+    sample_idx = np.arange(L, dtype=np.int64)[None, :]
+    column = np.arange(2 * CH, dtype=np.int64)[:, None]
+    freq = column // 2 + CH // 2
+    phase = (sample_idx * freq % L).astype(np.float32) * np.float32(2.0 * math.pi / L)
+    phase = phase.astype(np.float64)
+    values = np.where(column % 2 == 0, np.cos(phase), -np.sin(phase))
+    values = values.astype(np.float32).astype(jnp.bfloat16).astype(np.float32)
+    return (values * np.float32(L ** (-0.5))).astype(jnp.bfloat16)
+
+
+def exchange_kernel(
+    tm_n, chan_n, volt, taper, table, recv, vbuf, wide, filt, mid, send,
+    hist_sem, load_sem, own_sem, send_sem, recv_sem,
+):
+    inputs = volt.shape[0]
+    rows = 2 * CH // (tm_n * chan_n)
+    steps = SPEC_DEV // STEP
+    tm = lax.axis_index("tm")
+    chan = lax.axis_index("chan")
+    peers = tm_n * chan_n
+
+    def load_hist():
+        part = pl.ds(0, (TAPS - 1) * L)
+        return pltpu.make_async_copy(volt.at[:, part], vbuf.at[:, part], hist_sem)
+
+    def load_step(k):
+        start = pl.multiple_of((TAPS - 1 + STEP * k) * L, L)
+        part = pl.ds(start, STEP * L)
+        return pltpu.make_async_copy(volt.at[:, part], vbuf.at[:, part], load_sem.at[k])
+
+    load_hist().start()
+    for k in range(steps):
+        load_step(k).start()
+
+    def partner(j):
+        t = lax.rem(tm + j // chan_n, tm_n)
+        c = lax.rem(chan + lax.rem(j, chan_n), chan_n)
+        return t, c
+
+    barrier = pltpu.get_barrier_semaphore()
+
+    @pl.loop(1, peers)
+    def _(j):
+        t, c = partner(j)
+        pl.semaphore_signal(barrier, inc=1, device_id=(t, c), device_id_type=MESH)
+
+    for p in range(TAPS):
+        wide[p] = jnp.broadcast_to(taper[p : p + 1, :], (16, L))
+
+    load_hist().wait()
+    lanes = 256
+
+    @pl.loop(0, steps)
+    def _(k):
+        load_step(k).wait()
+
+        @pl.loop(0, STEP // GROUP)
+        def _(g):
+            first = k * STEP + g * GROUP
+
+            @pl.loop(0, inputs // 16)
+            def _(b):
+                r0 = pl.multiple_of(b * 16, 16)
+                for n0 in range(0, L, lanes):
+                    frames = []
+                    for f in range(GROUP + TAPS - 1):
+                        start = pl.multiple_of((first + f) * L + n0, 128)
+                        frames.append(vbuf[pl.ds(r0, 16), pl.ds(start, lanes)].astype(jnp.float32))
+                    weights = [wide[p, :, n0 : n0 + lanes] for p in range(TAPS)]
+                    for s in range(GROUP):
+                        total = weights[0] * frames[s]
+                        for p in range(1, TAPS):
+                            total = total + weights[p] * frames[s + p]
+                        filt[s, pl.ds(r0, 16), n0 : n0 + lanes] = total.astype(jnp.bfloat16)
+
+            for s in range(0, GROUP, 2):
+                pair = filt[s : s + 2].reshape(2 * inputs, L)
+                for h in range(0, 2 * CH, 256):
+                    out = lax.dot_general(
+                        table[h : h + 256], pair, (((1,), (1,)), ((), ())),
+                        preferred_element_type=jnp.float32,
+                    )
+                    for q in range(2):
+                        row = pl.multiple_of((g * GROUP + s + q) * (2 * CH), 2 * CH)
+                        mid[pl.ds(row + h, 256), :] = out[:, q * inputs : (q + 1) * inputs]
+
+        @pl.loop(0, 2 * CH // 8)
+        def _(b):
+            for u in range(8):
+                col = b * 8 + u
+                send[k, col] = mid[pl.ds(col, STEP, stride=2 * CH), :].astype(jnp.bfloat16)
+
+        @pl.when(k == 0)
+        def _():
+            pl.semaphore_wait(barrier, peers - 1)
+
+        where = pl.ds(pl.multiple_of(tm * SPEC_DEV + k * STEP, STEP), STEP)
+        columns = pl.ds(pl.multiple_of(chan * inputs, inputs), inputs)
+
+        @pl.loop(1, peers)
+        def _(j):
+            t, c = partner(j)
+            pltpu.make_async_remote_copy(
+                src_ref=send.at[k, pl.ds((t * chan_n + c) * rows, rows)],
+                dst_ref=recv.at[:, where, columns],
+                send_sem=send_sem.at[j],
+                recv_sem=recv_sem.at[j],
+                device_id=(t, c),
+                device_id_type=MESH,
+            ).start()
+
+        pltpu.make_async_copy(
+            send.at[k, pl.ds((tm * chan_n + chan) * rows, rows)],
+            recv.at[:, where, columns],
+            own_sem.at[k],
+        ).start()
+
+    where = pl.ds(pl.multiple_of(tm * SPEC_DEV, SPEC_DEV), SPEC_DEV)
+    columns = pl.ds(pl.multiple_of(chan * inputs, inputs), inputs)
+
+    @pl.loop(0, steps)
+    def _(k):
+        here = pl.ds(pl.multiple_of(tm * SPEC_DEV + k * STEP, STEP), STEP)
+        pltpu.make_async_copy(
+            send.at[k, pl.ds((tm * chan_n + chan) * rows, rows)],
+            recv.at[:, here, columns],
+            own_sem.at[k],
+        ).wait()
+
+    @pl.loop(1, peers)
+    def _(j):
+        t, c = partner(j)
+        whole = pltpu.make_async_remote_copy(
+            src_ref=recv.at[:, where, columns],
+            dst_ref=recv.at[:, where, columns],
+            send_sem=send_sem.at[j],
+            recv_sem=recv_sem.at[j],
+            device_id=(t, c),
+            device_id_type=MESH,
+        )
+        whole.wait_send()
+        whole.wait_recv()
+
+
+def exchange(voltages, taper_weights, tm_n, chan_n):
+    inputs = voltages.shape[0]
+    rows = 2 * CH // (tm_n * chan_n)
+    steps = SPEC_DEV // STEP
+    peers = tm_n * chan_n
+    table = jnp.asarray(table_rows())
+    return pl.pallas_call(
+        functools.partial(exchange_kernel, tm_n, chan_n),
+        out_shape=jax.ShapeDtypeStruct((rows, SPEC_DEV * tm_n, inputs * chan_n), jnp.bfloat16),
+        in_specs=[
+            pl.BlockSpec(memory_space=pl.ANY),
+            pl.BlockSpec(memory_space=pltpu.VMEM),
+            pl.BlockSpec(memory_space=pltpu.VMEM),
+        ],
+        out_specs=pl.BlockSpec(memory_space=pl.ANY),
+        scratch_shapes=[
+            pltpu.VMEM(voltages.shape, jnp.bfloat16),
+            pltpu.VMEM((TAPS, 16, L), jnp.float32),
+            pltpu.VMEM((GROUP, inputs, L), jnp.bfloat16),
+            pltpu.VMEM((STEP * 2 * CH, inputs), jnp.float32),
+            pltpu.VMEM((steps, 2 * CH, STEP, inputs), jnp.bfloat16),
+            pltpu.SemaphoreType.DMA,
+            pltpu.SemaphoreType.DMA((steps,)),
+            pltpu.SemaphoreType.DMA((steps,)),
+            pltpu.SemaphoreType.DMA((peers,)),
+            pltpu.SemaphoreType.DMA((peers,)),
+        ],
+        compiler_params=pltpu.CompilerParams(
+            collective_id=0, has_side_effects=True, vmem_limit_bytes=48 * MIB
+        ),
+        cost_estimate=pl.CostEstimate(
+            flops=4 * CH * L * inputs * SPEC_DEV, bytes_accessed=40 * MIB, transcendentals=0
+        ),
+    )(voltages, taper_weights, table)
+
+
+def correlate_kernel(scale, spec, out, left):
+    count = spec.shape[2]
+    depth = spec.shape[1]
+    tile = 256
+    for m in range(0, count, tile):
+        for r in range(2):
+            turned = spec[r, :, m : m + tile].T
+            left[0, m : m + tile, r * depth : (r + 1) * depth] = turned
+            left[1, m : m + tile, (1 - r) * depth : (2 - r) * depth] = turned if r else -turned
+    right = spec[...].reshape(2 * depth, count)
+    for part in range(2):
+        for m in range(0, count, tile):
+            block = lax.dot_general(
+                left[part, m : m + tile], right, (((1,), (0,)), ((), ())),
+                preferred_element_type=jnp.float32,
+            )
+            out[0, part, m : m + tile] = (block * scale).astype(jnp.bfloat16)
+
+
+def correlate_all(spectra):
+    rows, depth, count = spectra.shape
+    channels = rows // 2
+    return pl.pallas_call(
+        functools.partial(correlate_kernel, 1.0 / depth),
+        grid=(channels,),
+        out_shape=jax.ShapeDtypeStruct((channels, 2, count, count), jnp.bfloat16),
+        in_specs=[pl.BlockSpec((2, depth, count), lambda c: (c, 0, 0))],
+        out_specs=pl.BlockSpec((1, 2, count, count), lambda c: (c, 0, 0, 0)),
+        scratch_shapes=[pltpu.VMEM((2, count, 2 * depth), jnp.bfloat16)],
+        compiler_params=pltpu.CompilerParams(vmem_limit_bytes=48 * MIB),
+        cost_estimate=pl.CostEstimate(
+            flops=8 * channels * count * count * depth,
+            bytes_accessed=channels * count * (4 * count + 4 * depth),
+            transcendentals=0,
+        ),
+    )(spectra)
 
 
 def dft_table(length, channels):
@@ -34,9 +262,7 @@
     return contract(stacked, left_rows).reshape(2, count, count)
 
 
-def shards(voltages, taper_weights):
-    time_count = lax.axis_size("tm")
-    chan_count = lax.axis_size("chan")
+def shards_narrow(voltages, taper_weights, time_count, chan_count):
     inputs_here = voltages.shape[0]
     frame_count = SPEC_DEV + TAPS - 1
     frames = voltages.reshape(inputs_here, frame_count, L)
@@ -61,6 +287,14 @@
     return visibilities.astype(jnp.bfloat16)
 
 
+def shards(voltages, taper_weights):
+    time_count = lax.axis_size("tm")
+    chan_count = lax.axis_size("chan")
+    if voltages.shape[0] % 128 == 0:
+        return correlate_all(exchange(voltages, taper_weights, time_count, chan_count))
+    return shards_narrow(voltages, taper_weights, time_count, chan_count)
+
+
 def solution(mesh):
     placed = (P("chan", "tm"), P())
     return jax.shard_map(

time: 494 us -> 220 us (0.45)
  Pallas kernels: 0 us -> 217 us
  waiting for transfers between devices: 182 us -> 0 us
  local copies, waits for them, and re-layouts: 103 us -> 1.94 us
  blocking collectives: 100 us -> 0 us
  other arithmetic: 50.7 us -> 0 us
  matrix products: 47.4 us -> 0 us
  starting transfers between devices: 6.12 us -> 0 us
    pallas_call x0 -> x2, Pallas kernels: none -> 217 us  [the longest x1 194 us: exchange(): pl.pallas_call(functools.partial(exchange_kernel, tm_n, chan_n), out_shap...]
    all_to_all x1 -> x0, waiting for transfers between devices: 182 us -> none  [shards(): lax.all_to_all(turned, 'chan', split_axis=1, concat_axis=4, tiled=True)]
    all_to_all x1 -> x0, blocking collectives: 100 us -> none  [shards(): lax.all_to_all(spectra, 'tm', split_axis=0, concat_axis=5, tiled=True)]
    dot_general x9 -> x0, matrix products: 47.4 us -> none  [the longest x1 28.2 us: shards(): jnp.einsum('isn,nc->cis', filtered, table, preferred_element_type=jnp.flo...]
    convert_element_type x1 -> x0, other arithmetic: 32.7 us -> none  [shards(): return visibilities.astype(jnp.bfloat16)]
    dynamic_update_slice x8 -> x0, local copies, waits for them, and re-layouts: 32.5 us -> none  [shards(): visibilities = lax.map(correlate, flat) * scale]
    unnamed x1 -> x4, local copies, waits for them, and re-layouts: 23.5 us -> 1.94 us
    all_to_all x2 -> x0, local copies, waits for them, and re-layouts: 21.1 us -> none  [the longest x1 11.4 us: shards(): lax.all_to_all(turned, 'chan', split_axis=1, concat_axis=4, tiled=True)]
  transfers between devices with their start and end apart: 1 -> 0, of which waited for: 1 -> 0; matrix products, arithmetic and copies ran while one was open for 0% -> 0% of each run, Pallas kernels for 0% -> 0%
where the time goes in v1:
time: 220 us; the launch traced here: 219 us
  Pallas kernels  217 us (99%)
    pallas_call x1, Pallas kernels, exchange(): pl.pallas_call(functools.partial(exchange_kernel, tm_n, chan_n), out_shap...  194 us
    pallas_call x1, Pallas kernels, correlate_all(): pl.pallas_call(functools.partial(correlate_kernel, 1.0 / depth), grid=(ch...  22.3 us

profile of v1, /device:TPU:1, one launch (start us, length us, event | category | flops | bytes accessed | tf_op | source)
XLA Modules:
  0.0 218.6 jit_solution(15828617978010897460)
XLA Ops:
  0.0 0.0 copy-start
  0.0 0.7 copy-done
  0.7 0.0 copy-start.1
  0.7 1.2 copy-done.1
  1.9 194.4 %shard_map.37.spec = bf16[16,256,1024]{2,1,0:T(8,128)(2,1)} custom-call(bf16[128,68608]{1,0:T(8,128)(2,1)} %volt.1, f32[4,1024]{1,0:T(4,128)S(1)} %copy-done, bf16[512,1024]{1,0:T(8,128)(2,1)S(1)} %copy-done.1), custom_call_target="tpu_custom_call" | custom-call | flops 8589934592 | bytes 41943040 | tf_op jit(solution)/shard_map/pallas_call | solution.py:174
  196.3 22.3 %shard_map.38 = bf16[8,2,1024,1024]{3,2,1,0:T(8,128)(2,1)} custom-call(bf16[16,256,1024]{2,1,0:T(8,128)(2,1)} %shard_map.37.spec), custom_call_target="tpu_custom_call" | custom-call | flops 17179869184 | bytes 41943040 | tf_op jit(solution)/shard_map/pallas_call | solution.py:226
Async XLA Ops:
  0.0 0.7 copy-start
  0.7 1.2 copy-start.1

commit v2 on v1

--- a/solution.py
+++ b/solution.py
@@ -41,6 +41,7 @@
     tm = lax.axis_index("tm")
     chan = lax.axis_index("chan")
     peers = tm_n * chan_n
+    me = tm * chan_n + chan
 
     def load_hist():
         part = pl.ds(0, (TAPS - 1) * L)
@@ -117,45 +118,42 @@
         def _():
             pl.semaphore_wait(barrier, peers - 1)
 
-        where = pl.ds(pl.multiple_of(tm * SPEC_DEV + k * STEP, STEP), STEP)
-        columns = pl.ds(pl.multiple_of(chan * inputs, inputs), inputs)
-
-        @pl.loop(1, peers)
-        def _(j):
-            t, c = partner(j)
-            pltpu.make_async_remote_copy(
-                src_ref=send.at[k, pl.ds((t * chan_n + c) * rows, rows)],
-                dst_ref=recv.at[:, where, columns],
-                send_sem=send_sem.at[j],
-                recv_sem=recv_sem.at[j],
-                device_id=(t, c),
-                device_id_type=MESH,
-            ).start()
+        @pl.loop(0, peers)
+        def _(n):
+            far = lax.rem(lax.rem(n, chan_n) + 2 * tm + chan_n // 2, chan_n)
+            j = n // chan_n * chan_n + far
+
+            @pl.when(j != 0)
+            def _():
+                t, c = partner(j)
+                pltpu.make_async_remote_copy(
+                    src_ref=send.at[k, pl.ds((t * chan_n + c) * rows, rows)],
+                    dst_ref=recv.at[me, k],
+                    send_sem=send_sem.at[j],
+                    recv_sem=recv_sem.at[j],
+                    device_id=(t, c),
+                    device_id_type=MESH,
+                ).start()
 
         pltpu.make_async_copy(
-            send.at[k, pl.ds((tm * chan_n + chan) * rows, rows)],
-            recv.at[:, where, columns],
-            own_sem.at[k],
+            send.at[k, pl.ds(me * rows, rows)], recv.at[me, k], own_sem.at[k]
         ).start()
-
-    where = pl.ds(pl.multiple_of(tm * SPEC_DEV, SPEC_DEV), SPEC_DEV)
-    columns = pl.ds(pl.multiple_of(chan * inputs, inputs), inputs)
 
     @pl.loop(0, steps)
     def _(k):
-        here = pl.ds(pl.multiple_of(tm * SPEC_DEV + k * STEP, STEP), STEP)
         pltpu.make_async_copy(
-            send.at[k, pl.ds((tm * chan_n + chan) * rows, rows)],
-            recv.at[:, here, columns],
-            own_sem.at[k],
+            send.at[k, pl.ds(me * rows, rows)], recv.at[me, k], own_sem.at[k]
         ).wait()
 
     @pl.loop(1, peers)
     def _(j):
         t, c = partner(j)
+        source = lax.rem(tm + tm_n - j // chan_n, tm_n) * chan_n + lax.rem(
+            chan + chan_n - lax.rem(j, chan_n), chan_n
+        )
         whole = pltpu.make_async_remote_copy(
-            src_ref=recv.at[:, where, columns],
-            dst_ref=recv.at[:, where, columns],
+            src_ref=recv.at[source],
+            dst_ref=recv.at[source],
             send_sem=send_sem.at[j],
             recv_sem=recv_sem.at[j],
             device_id=(t, c),
@@ -173,7 +171,7 @@
     table = jnp.asarray(table_rows())
     return pl.pallas_call(
         functools.partial(exchange_kernel, tm_n, chan_n),
-        out_shape=jax.ShapeDtypeStruct((rows, SPEC_DEV * tm_n, inputs * chan_n), jnp.bfloat16),
+        out_shape=jax.ShapeDtypeStruct((peers, steps, rows, STEP, inputs), jnp.bfloat16),
         in_specs=[
             pl.BlockSpec(memory_space=pl.ANY),
             pl.BlockSpec(memory_space=pltpu.VMEM),
@@ -201,35 +199,41 @@
     )(voltages, taper_weights, table)
 
 
-def correlate_kernel(scale, spec, out, left):
-    count = spec.shape[2]
-    depth = spec.shape[1]
+def correlate_kernel(chan_n, scale, spec, out, right):
+    peers, steps, _, step, inputs = spec.shape
+    depth = right.shape[0] // 2
+    for p in range(peers):
+        t, g = p // chan_n, p % chan_n
+        for k in range(steps):
+            for r in range(2):
+                first = r * depth + (t * steps + k) * step
+                right[first : first + step, g * inputs : (g + 1) * inputs] = spec[p, k, r]
+    count = right.shape[1]
     tile = 256
     for m in range(0, count, tile):
-        for r in range(2):
-            turned = spec[r, :, m : m + tile].T
-            left[0, m : m + tile, r * depth : (r + 1) * depth] = turned
-            left[1, m : m + tile, (1 - r) * depth : (2 - r) * depth] = turned if r else -turned
-    right = spec[...].reshape(2 * depth, count)
-    for part in range(2):
-        for m in range(0, count, tile):
-            block = lax.dot_general(
-                left[part, m : m + tile], right, (((1,), (0,)), ((), ())),
-                preferred_element_type=jnp.float32,
-            )
-            out[0, part, m : m + tile] = (block * scale).astype(jnp.bfloat16)
-
-
-def correlate_all(spectra):
-    rows, depth, count = spectra.shape
+        turned = right[:, m : m + tile].T
+        other = jnp.concatenate([turned[:, depth:], -turned[:, :depth]], axis=1)
+        both = jnp.concatenate([turned, other], axis=0)
+        block = lax.dot_general(
+            both, right[...], (((1,), (0,)), ((), ())), preferred_element_type=jnp.float32
+        )
+        block = (block * scale).astype(jnp.bfloat16)
+        out[0, 0, m : m + tile] = block[:tile]
+        out[0, 1, m : m + tile] = block[tile:]
+
+
+def correlate_all(spectra, chan_n):
+    peers, steps, rows, step, inputs = spectra.shape
     channels = rows // 2
+    depth = peers // chan_n * steps * step
+    count = chan_n * inputs
     return pl.pallas_call(
-        functools.partial(correlate_kernel, 1.0 / depth),
+        functools.partial(correlate_kernel, chan_n, 1.0 / depth),
         grid=(channels,),
         out_shape=jax.ShapeDtypeStruct((channels, 2, count, count), jnp.bfloat16),
-        in_specs=[pl.BlockSpec((2, depth, count), lambda c: (c, 0, 0))],
+        in_specs=[pl.BlockSpec((peers, steps, 2, step, inputs), lambda c: (0, 0, c, 0, 0))],
         out_specs=pl.BlockSpec((1, 2, count, count), lambda c: (c, 0, 0, 0)),
-        scratch_shapes=[pltpu.VMEM((2, count, 2 * depth), jnp.bfloat16)],
+        scratch_shapes=[pltpu.VMEM((2 * depth, count), jnp.bfloat16)],
         compiler_params=pltpu.CompilerParams(vmem_limit_bytes=48 * MIB),
         cost_estimate=pl.CostEstimate(
             flops=8 * channels * count * count * depth,
@@ -291,7 +295,7 @@
     time_count = lax.axis_size("tm")
     chan_count = lax.axis_size("chan")
     if voltages.shape[0] % 128 == 0:
-        return correlate_all(exchange(voltages, taper_weights, time_count, chan_count))
+        return correlate_all(exchange(voltages, taper_weights, time_count, chan_count), chan_count)
     return shards_narrow(voltages, taper_weights, time_count, chan_count)
 
 

time: 220 us -> 221 us (level)
  no operation moved by 1% of the time
where the time goes in v2:
time: 221 us; the launch traced here: 219 us
  Pallas kernels  217 us (98%)
    pallas_call x1, Pallas kernels, exchange(): pl.pallas_call(functools.partial(exchange_kernel, tm_n, chan_n), out_shap...  194 us
    pallas_call x1, Pallas kernels, correlate_all(): pl.pallas_call(functools.partial(correlate_kernel, chan_n, 1.0 / depth),...  23.1 us

profile of v2, /device:TPU:1, one launch (start us, length us, event | category | flops | bytes accessed | tf_op | source)
XLA Modules:
  0.0 219.4 jit_solution(9274402246587722374)
XLA Ops:
  0.0 0.0 copy-start
  0.0 0.7 copy-done
  0.7 0.0 copy-start.1
  0.7 1.2 copy-done.1
  1.9 194.4 %shard_map.37.spec = bf16[32,4,16,16,128]{4,3,2,1,0:T(8,128)(2,1)} custom-call(bf16[128,68608]{1,0:T(8,128)(2,1)} %volt.1, f32[4,1024]{1,0:T(4,128)S(1)} %copy-done, bf16[512,1024]{1,0:T(8,128)(2,1)S(1)} %copy-done.1), custom_call_target="tpu_custom_call" | custom-call | flops 8589934592 | bytes 41943040 | tf_op jit(solution)/shard_map/pallas_call | solution.py:172
  196.4 23.1 %shard_map.38 = bf16[8,2,1024,1024]{3,2,1,0:T(8,128)(2,1)} custom-call(bf16[32,4,16,16,128]{4,3,2,1,0:T(8,128)(2,1)} %shard_map.37.spec), custom_call_target="tpu_custom_call" | custom-call | flops 17179869184 | bytes 41943040 | tf_op jit(solution)/shard_map/pallas_call | solution.py:230
Async XLA Ops:
  0.0 0.7 copy-start
  0.7 1.2 copy-start.1

commit v3 on v2

--- a/solution.py
+++ b/solution.py
@@ -32,8 +32,8 @@
 
 
 def exchange_kernel(
-    tm_n, chan_n, volt, taper, table, recv, vbuf, wide, filt, mid, send,
-    hist_sem, load_sem, own_sem, send_sem, recv_sem,
+    tm_n, chan_n, early, scale, volt, taper, table, late, done, vbuf, wide, filt, mid, send,
+    soon, right, made, hist_sem, load_sem, own_sem, send_sem, recv_sem, made_sem,
 ):
     inputs = volt.shape[0]
     rows = 2 * CH // (tm_n * chan_n)
@@ -42,6 +42,7 @@
     chan = lax.axis_index("chan")
     peers = tm_n * chan_n
     me = tm * chan_n + chan
+    spread = chan_n // 2 + 2 * tm
 
     def load_hist():
         part = pl.ds(0, (TAPS - 1) * L)
@@ -53,8 +54,7 @@
         return pltpu.make_async_copy(volt.at[:, part], vbuf.at[:, part], load_sem.at[k])
 
     load_hist().start()
-    for k in range(steps):
-        load_step(k).start()
+    load_step(0).start()
 
     def partner(j):
         t = lax.rem(tm + j // chan_n, tm_n)
@@ -77,6 +77,10 @@
     @pl.loop(0, steps)
     def _(k):
         load_step(k).wait()
+
+        @pl.when(k + 1 < steps)
+        def _():
+            load_step(k + 1).start()
 
         @pl.loop(0, STEP // GROUP)
         def _(g):
@@ -120,86 +124,83 @@
 
         @pl.loop(0, peers)
         def _(n):
-            far = lax.rem(lax.rem(n, chan_n) + 2 * tm + chan_n // 2, chan_n)
-            j = n // chan_n * chan_n + far
+            j = lax.rem(n + spread, peers)
 
             @pl.when(j != 0)
             def _():
                 t, c = partner(j)
                 pltpu.make_async_remote_copy(
-                    src_ref=send.at[k, pl.ds((t * chan_n + c) * rows, rows)],
-                    dst_ref=recv.at[me, k],
-                    send_sem=send_sem.at[j],
-                    recv_sem=recv_sem.at[j],
+                    src_ref=send.at[k, pl.ds((t * chan_n + c) * rows, early)],
+                    dst_ref=soon.at[me, k],
+                    send_sem=send_sem.at[0, j],
+                    recv_sem=recv_sem.at[0, j],
                     device_id=(t, c),
                     device_id_type=MESH,
                 ).start()
 
-        pltpu.make_async_copy(
-            send.at[k, pl.ds(me * rows, rows)], recv.at[me, k], own_sem.at[k]
-        ).start()
-
-    @pl.loop(0, steps)
-    def _(k):
-        pltpu.make_async_copy(
-            send.at[k, pl.ds(me * rows, rows)], recv.at[me, k], own_sem.at[k]
-        ).wait()
-
-    @pl.loop(1, peers)
-    def _(j):
-        t, c = partner(j)
-        source = lax.rem(tm + tm_n - j // chan_n, tm_n) * chan_n + lax.rem(
-            chan + chan_n - lax.rem(j, chan_n), chan_n
-        )
-        whole = pltpu.make_async_remote_copy(
-            src_ref=recv.at[source],
-            dst_ref=recv.at[source],
-            send_sem=send_sem.at[j],
-            recv_sem=recv_sem.at[j],
-            device_id=(t, c),
-            device_id_type=MESH,
-        )
-        whole.wait_send()
-        whole.wait_recv()
-
-
-def exchange(voltages, taper_weights, tm_n, chan_n):
-    inputs = voltages.shape[0]
-    rows = 2 * CH // (tm_n * chan_n)
-    steps = SPEC_DEV // STEP
-    peers = tm_n * chan_n
-    table = jnp.asarray(table_rows())
-    return pl.pallas_call(
-        functools.partial(exchange_kernel, tm_n, chan_n),
-        out_shape=jax.ShapeDtypeStruct((peers, steps, rows, STEP, inputs), jnp.bfloat16),
-        in_specs=[
-            pl.BlockSpec(memory_space=pl.ANY),
-            pl.BlockSpec(memory_space=pltpu.VMEM),
-            pl.BlockSpec(memory_space=pltpu.VMEM),
-        ],
-        out_specs=pl.BlockSpec(memory_space=pl.ANY),
-        scratch_shapes=[
-            pltpu.VMEM(voltages.shape, jnp.bfloat16),
-            pltpu.VMEM((TAPS, 16, L), jnp.float32),
-            pltpu.VMEM((GROUP, inputs, L), jnp.bfloat16),
-            pltpu.VMEM((STEP * 2 * CH, inputs), jnp.float32),
-            pltpu.VMEM((steps, 2 * CH, STEP, inputs), jnp.bfloat16),
-            pltpu.SemaphoreType.DMA,
-            pltpu.SemaphoreType.DMA((steps,)),
-            pltpu.SemaphoreType.DMA((steps,)),
-            pltpu.SemaphoreType.DMA((peers,)),
-            pltpu.SemaphoreType.DMA((peers,)),
-        ],
-        compiler_params=pltpu.CompilerParams(
-            collective_id=0, has_side_effects=True, vmem_limit_bytes=48 * MIB
-        ),
-        cost_estimate=pl.CostEstimate(
-            flops=4 * CH * L * inputs * SPEC_DEV, bytes_accessed=40 * MIB, transcendentals=0
-        ),
-    )(voltages, taper_weights, table)
-
-
-def correlate_kernel(chan_n, scale, spec, out, right):
+    own_soon = pltpu.make_async_copy(
+        send.at[:, pl.ds(me * rows, early)], soon.at[me], own_sem.at[0]
+    )
+    own_late = pltpu.make_async_copy(
+        send.at[:, pl.ds(me * rows + early, rows - early)], late.at[me], own_sem.at[1]
+    )
+    own_soon.start()
+    own_late.start()
+
+    @pl.loop(0, peers)
+    def _(n):
+        j = lax.rem(n + spread, peers)
+
+        @pl.when(j != 0)
+        def _():
+            t, c = partner(j)
+            pltpu.make_async_remote_copy(
+                src_ref=send.at[:, pl.ds((t * chan_n + c) * rows + early, rows - early)],
+                dst_ref=late.at[me],
+                send_sem=send_sem.at[1, j],
+                recv_sem=recv_sem.at[1, j],
+                device_id=(t, c),
+                device_id_type=MESH,
+            ).start()
+
+    def finish(part, land):
+        @pl.loop(1, peers)
+        def _(j):
+            t, c = partner(j)
+            source = lax.rem(tm + tm_n - j // chan_n, tm_n) * chan_n + lax.rem(
+                chan + chan_n - lax.rem(j, chan_n), chan_n
+            )
+            whole = pltpu.make_async_remote_copy(
+                src_ref=land.at[source],
+                dst_ref=land.at[source],
+                send_sem=send_sem.at[part, j],
+                recv_sem=recv_sem.at[part, j],
+                device_id=(t, c),
+                device_id_type=MESH,
+            )
+            whole.wait_send()
+            whole.wait_recv()
+
+    own_soon.wait()
+    finish(0, soon)
+
+    @pl.loop(0, early // 2)
+    def _(c):
+        gather_rows(chan_n, soon, 2 * c, right)
+        for m in range(0, right.shape[1], TILE):
+            made[:, m : m + TILE] = correlate_tile(right, m, scale)
+        written = pltpu.make_async_copy(made, done.at[c], made_sem)
+        written.start()
+        written.wait()
+
+    own_late.wait()
+    finish(1, late)
+
+
+TILE = 256
+
+
+def gather_rows(chan_n, spec, row, right):
     peers, steps, _, step, inputs = spec.shape
     depth = right.shape[0] // 2
     for p in range(peers):
@@ -207,40 +208,136 @@
         for k in range(steps):
             for r in range(2):
                 first = r * depth + (t * steps + k) * step
-                right[first : first + step, g * inputs : (g + 1) * inputs] = spec[p, k, r]
-    count = right.shape[1]
-    tile = 256
-    for m in range(0, count, tile):
-        turned = right[:, m : m + tile].T
-        other = jnp.concatenate([turned[:, depth:], -turned[:, :depth]], axis=1)
-        both = jnp.concatenate([turned, other], axis=0)
-        block = lax.dot_general(
-            both, right[...], (((1,), (0,)), ((), ())), preferred_element_type=jnp.float32
+                right[first : first + step, g * inputs : (g + 1) * inputs] = spec[p, k, row + r]
+
+
+def correlate_tile(right, m, scale):
+    depth = right.shape[0] // 2
+    turned = right[:, m : m + TILE].T
+    other = jnp.concatenate([turned[:, depth:], -turned[:, :depth]], axis=1)
+    both = jnp.concatenate([turned, other], axis=0)
+    block = lax.dot_general(
+        both, right[...], (((1,), (0,)), ((), ())), preferred_element_type=jnp.float32
+    )
+    return (block * scale).astype(jnp.bfloat16).reshape(2, TILE, right.shape[1])
+
+
+def exchange(voltages, taper_weights, tm_n, chan_n):
+    inputs = voltages.shape[0]
+    rows = 2 * CH // (tm_n * chan_n)
+    steps = SPEC_DEV // STEP
+    peers = tm_n * chan_n
+    depth = SPEC_DEV * tm_n
+    count = inputs * chan_n
+    early = 2 * (3 * rows // 16)
+    table = jnp.asarray(table_rows())
+    return pl.pallas_call(
+        functools.partial(exchange_kernel, tm_n, chan_n, early, 1.0 / depth),
+        out_shape=(
+            jax.ShapeDtypeStruct((peers, steps, rows - early, STEP, inputs), jnp.bfloat16),
+            jax.ShapeDtypeStruct((early // 2, 2, count, count), jnp.bfloat16),
+        ),
+        in_specs=[
+            pl.BlockSpec(memory_space=pl.ANY),
+            pl.BlockSpec(memory_space=pltpu.VMEM),
+            pl.BlockSpec(memory_space=pltpu.VMEM),
+        ],
+        out_specs=(pl.BlockSpec(memory_space=pl.ANY), pl.BlockSpec(memory_space=pl.ANY)),
+        scratch_shapes=[
+            pltpu.VMEM(voltages.shape, jnp.bfloat16),
+            pltpu.VMEM((TAPS, 16, L), jnp.float32),
+            pltpu.VMEM((GROUP, inputs, L), jnp.bfloat16),
+            pltpu.VMEM((STEP * 2 * CH, inputs), jnp.float32),
+            pltpu.VMEM((steps, 2 * CH, STEP, inputs), jnp.bfloat16),
+            pltpu.VMEM((peers, steps, early, STEP, inputs), jnp.bfloat16),
+            pltpu.VMEM((2 * depth, count), jnp.bfloat16),
+            pltpu.VMEM((2, count, count), jnp.bfloat16),
+            pltpu.SemaphoreType.DMA,
+            pltpu.SemaphoreType.DMA((steps,)),
+            pltpu.SemaphoreType.DMA((2,)),
+            pltpu.SemaphoreType.DMA((2, peers)),
+            pltpu.SemaphoreType.DMA((2, peers)),
+            pltpu.SemaphoreType.DMA,
+        ],
+        compiler_params=pltpu.CompilerParams(
+            collective_id=0, has_side_effects=True, vmem_limit_bytes=60 * MIB
+        ),
+        cost_estimate=pl.CostEstimate(
+            flops=4 * CH * L * inputs * SPEC_DEV, bytes_accessed=40 * MIB, transcendentals=0
+        ),
+    )(voltages, taper_weights, table)
+
+
+def correlate_kernel(chan_n, scale, spec, done, out, right, made, done_sem, made_sem):
+    c = pl.program_id(0)
+    last = pl.num_programs(0) - 1
+    ready = done.shape[0]
+    tiles = right.shape[1] // TILE
+
+    def hand_on(d):
+        return pltpu.make_async_copy(done.at[d], out.at[d], done_sem.at[d])
+
+    def write(channel, i):
+        slot = lax.rem(channel, 2)
+        part = pl.ds(i * TILE, TILE)
+        return pltpu.make_async_copy(
+            made.at[slot, :, part], out.at[ready + channel, :, part], made_sem.at[slot, i]
         )
-        block = (block * scale).astype(jnp.bfloat16)
-        out[0, 0, m : m + tile] = block[:tile]
-        out[0, 1, m : m + tile] = block[tile:]
-
-
-def correlate_all(spectra, chan_n):
+
+    @pl.when(c == 0)
+    def _():
+        for d in range(ready):
+            hand_on(d).start()
+
+    gather_rows(chan_n, spec, 0, right)
+    for i in range(tiles):
+        @pl.when(c >= 2)
+        def _():
+            write(c - 2, i).wait()
+
+        made[lax.rem(c, 2), :, i * TILE : (i + 1) * TILE] = correlate_tile(right, i * TILE, scale)
+        write(c, i).start()
+
+    @pl.when(c == last)
+    def _():
+        for i in range(tiles):
+            @pl.when(c >= 1)
+            def _():
+                write(c - 1, i).wait()
+
+            write(c, i).wait()
+        for d in range(ready):
+            hand_on(d).wait()
+
+
+def correlate_all(spectra, done, chan_n):
     peers, steps, rows, step, inputs = spectra.shape
     channels = rows // 2
+    ready = done.shape[0]
     depth = peers // chan_n * steps * step
     count = chan_n * inputs
     return pl.pallas_call(
         functools.partial(correlate_kernel, chan_n, 1.0 / depth),
         grid=(channels,),
-        out_shape=jax.ShapeDtypeStruct((channels, 2, count, count), jnp.bfloat16),
-        in_specs=[pl.BlockSpec((peers, steps, 2, step, inputs), lambda c: (0, 0, c, 0, 0))],
-        out_specs=pl.BlockSpec((1, 2, count, count), lambda c: (c, 0, 0, 0)),
-        scratch_shapes=[pltpu.VMEM((2 * depth, count), jnp.bfloat16)],
-        compiler_params=pltpu.CompilerParams(vmem_limit_bytes=48 * MIB),
+        out_shape=jax.ShapeDtypeStruct((ready + channels, 2, count, count), jnp.bfloat16),
+        in_specs=[
+            pl.BlockSpec((peers, steps, 2, step, inputs), lambda c: (0, 0, c, 0, 0)),
+            pl.BlockSpec(memory_space=pl.ANY),
+        ],
+        out_specs=pl.BlockSpec(memory_space=pl.ANY),
+        scratch_shapes=[
+            pltpu.VMEM((2 * depth, count), jnp.bfloat16),
+            pltpu.VMEM((2, 2, count, count), jnp.bfloat16),
+            pltpu.SemaphoreType.DMA((ready,)),
+            pltpu.SemaphoreType.DMA((2, count // TILE)),
+        ],
+        compiler_params=pltpu.CompilerParams(vmem_limit_bytes=60 * MIB),
         cost_estimate=pl.CostEstimate(
             flops=8 * channels * count * count * depth,
             bytes_accessed=channels * count * (4 * count + 4 * depth),
             transcendentals=0,
         ),
-    )(spectra)
+    )(spectra, done)
 
 
 def dft_table(length, channels):
@@ -295,7 +392,8 @@
     time_count = lax.axis_size("tm")
     chan_count = lax.axis_size("chan")
     if voltages.shape[0] % 128 == 0:
-        return correlate_all(exchange(voltages, taper_weights, time_count, chan_count), chan_count)
+        late, done = exchange(voltages, taper_weights, time_count, chan_count)
+        return correlate_all(late, done, chan_count)
     return shards_narrow(voltages, taper_weights, time_count, chan_count)
 
 

time: 221 us -> 583 us (2.64)
  Pallas kernels: 217 us -> 577 us
    pallas_call x1, Pallas kernels: 23.1 us -> 384 us  [correlate_all(): pl.pallas_call(functools.partial(correlate_kernel, chan_n, 1.0 / depth),...]
where the time goes in v3:
time: 583 us; the launch traced here: 577 us
  Pallas kernels  577 us (99%)
    pallas_call x1, Pallas kernels, correlate_all(): pl.pallas_call(functools.partial(correlate_kernel, chan_n, 1.0 / depth),...  384 us
    pallas_call x1, Pallas kernels, exchange(): pl.pallas_call(functools.partial(exchange_kernel, tm_n, chan_n, early, 1....  194 us

profile of v3, /device:TPU:1, one launch (start us, length us, event | category | flops | bytes accessed | tf_op | source)
XLA Modules:
  0.0 577.1 jit_solution(9463470614660558423)
XLA Ops:
  0.0 193.5 %shard_map.37 = (bf16[32,4,10,16,128]{4,3,2,1,0:T(8,128)(2,1)}, bf16[3,2,1024,1024]{3,2,1,0:T(8,128)(2,1)}) custom-call(bf16[128,68608]{1,0:T(8,128)(2,1)} %volt.1, f32[4,1024]{1,0:T(4,128)} %taper.1, bf16[512,1024]{1,0:T(8,128)(2,1)} %constant.2.clone.table), custom_call_target="tpu_custom_call" | custom-call | flops 8589934592 | bytes 41943040 | tf_op jit(solution)/shard_map/pallas_call | solution.py:234
  193.5 383.6 %shard_map.38 = bf16[8,2,1024,1024]{3,2,1,0:T(8,128)(2,1)} custom-call(bf16[32,4,10,16,128]{4,3,2,1,0:T(8,128)(2,1)} %get-tuple-element.7.spec, bf16[3,2,1024,1024]{3,2,1,0:T(8,128)(2,1)} %get-tuple-element.8.done), custom_call_target="tpu_custom_call" | custom-call | flops 10737418240 | bytes 26214400 | tf_op jit(solution)/shard_map/pallas_call | solution.py:319

commit v4 on v3

--- a/solution.py
+++ b/solution.py
@@ -42,7 +42,6 @@
     chan = lax.axis_index("chan")
     peers = tm_n * chan_n
     me = tm * chan_n + chan
-    spread = chan_n // 2 + 2 * tm
 
     def load_hist():
         part = pl.ds(0, (TAPS - 1) * L)
@@ -60,6 +59,11 @@
         t = lax.rem(tm + j // chan_n, tm_n)
         c = lax.rem(chan + lax.rem(j, chan_n), chan_n)
         return t, c
+
+    def order(n):
+        half = chan_n // 2
+        far = lax.rem(n, 2) * half + lax.rem(n, chan_n) // 2
+        return n // chan_n * chan_n + lax.rem(far + 2 * tm, chan_n)
 
     barrier = pltpu.get_barrier_semaphore()
 
@@ -124,7 +128,7 @@
 
         @pl.loop(0, peers)
         def _(n):
-            j = lax.rem(n + spread, peers)
+            j = order(n)
 
             @pl.when(j != 0)
             def _():
@@ -149,7 +153,7 @@
 
     @pl.loop(0, peers)
     def _(n):
-        j = lax.rem(n + spread, peers)
+        j = order(n)
 
         @pl.when(j != 0)
         def _():
@@ -268,14 +272,17 @@
     )(voltages, taper_weights, table)
 
 
-def correlate_kernel(chan_n, scale, spec, done, out, right, made, done_sem, made_sem):
+def correlate_kernel(chan_n, channels, scale, spec, done, out, right, made, passing, in_sem, out_sem, made_sem):
     c = pl.program_id(0)
-    last = pl.num_programs(0) - 1
+    last = channels - 1
     ready = done.shape[0]
     tiles = right.shape[1] // TILE
 
+    def take(d):
+        return pltpu.make_async_copy(done.at[d], passing.at[d], in_sem.at[d])
+
     def hand_on(d):
-        return pltpu.make_async_copy(done.at[d], out.at[d], done_sem.at[d])
+        return pltpu.make_async_copy(passing.at[d], out.at[d], out_sem.at[d])
 
     def write(channel, i):
         slot = lax.rem(channel, 2)
@@ -287,6 +294,12 @@
     @pl.when(c == 0)
     def _():
         for d in range(ready):
+            take(d).start()
+
+    for d in range(ready):
+        @pl.when(c == min(d + 1, channels - 1))
+        def _():
+            take(d).wait()
             hand_on(d).start()
 
     gather_rows(chan_n, spec, 0, right)
@@ -317,7 +330,7 @@
     depth = peers // chan_n * steps * step
     count = chan_n * inputs
     return pl.pallas_call(
-        functools.partial(correlate_kernel, chan_n, 1.0 / depth),
+        functools.partial(correlate_kernel, chan_n, channels, 1.0 / depth),
         grid=(channels,),
         out_shape=jax.ShapeDtypeStruct((ready + channels, 2, count, count), jnp.bfloat16),
         in_specs=[
@@ -328,6 +341,8 @@
         scratch_shapes=[
             pltpu.VMEM((2 * depth, count), jnp.bfloat16),
             pltpu.VMEM((2, 2, count, count), jnp.bfloat16),
+            pltpu.VMEM((ready, 2, count, count), jnp.bfloat16),
+            pltpu.SemaphoreType.DMA((ready,)),
             pltpu.SemaphoreType.DMA((ready,)),
             pltpu.SemaphoreType.DMA((2, count // TILE)),
         ],

time: 583 us -> 221 us (0.38)
  Pallas kernels: 577 us -> 221 us
    pallas_call x1, Pallas kernels: 384 us -> 21.4 us  [correlate_all(): pl.pallas_call(functools.partial(correlate_kernel, chan_n, channels, 1.0...]
    pallas_call x1, Pallas kernels: 194 us -> 199 us  [exchange(): pl.pallas_call(functools.partial(exchange_kernel, tm_n, chan_n, early, 1....]
where the time goes in v4:
time: 221 us
  Pallas kernels  221 us (100%)
    pallas_call x1, Pallas kernels, exchange(): pl.pallas_call(functools.partial(exchange_kernel, tm_n, chan_n, early, 1....  199 us
    pallas_call x1, Pallas kernels, correlate_all(): pl.pallas_call(functools.partial(correlate_kernel, chan_n, channels, 1.0...  21.4 us

profile of v4, /device:TPU:1, one launch (start us, length us, event | category | flops | bytes accessed | tf_op | source)
XLA Modules:
  0.0 220.9 jit_solution(17910292354776810175)
XLA Ops:
  0.0 199.5 %shard_map.37 = (bf16[32,4,10,16,128]{4,3,2,1,0:T(8,128)(2,1)}, bf16[3,2,1024,1024]{3,2,1,0:T(8,128)(2,1)}) custom-call(bf16[128,68608]{1,0:T(8,128)(2,1)} %volt.1, f32[4,1024]{1,0:T(4,128)} %taper.1, bf16[512,1024]{1,0:T(8,128)(2,1)} %constant.2.clone.table), custom_call_target="tpu_custom_call" | custom-call | flops 8589934592 | bytes 41943040 | tf_op jit(solution)/shard_map/pallas_call | solution.py:238
  199.5 21.4 %shard_map.38 = bf16[8,2,1024,1024]{3,2,1,0:T(8,128)(2,1)} custom-call(bf16[32,4,10,16,128]{4,3,2,1,0:T(8,128)(2,1)} %get-tuple-element.7.spec, bf16[3,2,1024,1024]{3,2,1,0:T(8,128)(2,1)} %get-tuple-element.8.done), custom_call_target="tpu_custom_call" | custom-call | flops 10737418240 | bytes 26214400 | tf_op jit(solution)/shard_map/pallas_call | solution.py:332

commit v5 on v4

--- a/solution.py
+++ b/solution.py
@@ -32,8 +32,8 @@
 
 
 def exchange_kernel(
-    tm_n, chan_n, early, scale, volt, taper, table, late, done, vbuf, wide, filt, mid, send,
-    soon, right, made, hist_sem, load_sem, own_sem, send_sem, recv_sem, made_sem,
+    tm_n, chan_n, early, scale, volt, taper, table_in, late, done, table, vbuf, wide, filt, mid, send,
+    soon, right, made, table_sem, hist_sem, load_sem, own_sem, send_sem, recv_sem, made_sem,
 ):
     inputs = volt.shape[0]
     rows = 2 * CH // (tm_n * chan_n)
@@ -52,8 +52,10 @@
         part = pl.ds(start, STEP * L)
         return pltpu.make_async_copy(volt.at[:, part], vbuf.at[:, part], load_sem.at[k])
 
+    load_table = pltpu.make_async_copy(table_in, table, table_sem)
     load_hist().start()
     load_step(0).start()
+    load_table.start()
 
     def partner(j):
         t = lax.rem(tm + j // chan_n, tm_n)
@@ -76,6 +78,7 @@
         wide[p] = jnp.broadcast_to(taper[p : p + 1, :], (16, L))
 
     load_hist().wait()
+    load_table.wait()
     lanes = 256
 
     @pl.loop(0, steps)
@@ -233,7 +236,7 @@
     peers = tm_n * chan_n
     depth = SPEC_DEV * tm_n
     count = inputs * chan_n
-    early = 2 * (3 * rows // 16)
+    early = 2 * (rows // 8)
     table = jnp.asarray(table_rows())
     return pl.pallas_call(
         functools.partial(exchange_kernel, tm_n, chan_n, early, 1.0 / depth),
@@ -244,10 +247,11 @@
         in_specs=[
             pl.BlockSpec(memory_space=pl.ANY),
             pl.BlockSpec(memory_space=pltpu.VMEM),
-            pl.BlockSpec(memory_space=pltpu.VMEM),
+            pl.BlockSpec(memory_space=pl.ANY),
         ],
         out_specs=(pl.BlockSpec(memory_space=pl.ANY), pl.BlockSpec(memory_space=pl.ANY)),
         scratch_shapes=[
+            pltpu.VMEM(table.shape, jnp.bfloat16),
             pltpu.VMEM(voltages.shape, jnp.bfloat16),
             pltpu.VMEM((TAPS, 16, L), jnp.float32),
             pltpu.VMEM((GROUP, inputs, L), jnp.bfloat16),
@@ -256,6 +260,7 @@
             pltpu.VMEM((peers, steps, early, STEP, inputs), jnp.bfloat16),
             pltpu.VMEM((2 * depth, count), jnp.bfloat16),
             pltpu.VMEM((2, count, count), jnp.bfloat16),
+            pltpu.SemaphoreType.DMA,
             pltpu.SemaphoreType.DMA,
             pltpu.SemaphoreType.DMA((steps,)),
             pltpu.SemaphoreType.DMA((2,)),

time: 221 us -> 221 us (level)
  no operation moved by 1% of the time
where the time goes in v5:
time: 221 us
  Pallas kernels  221 us (100%)
    pallas_call x1, Pallas kernels, exchange(): pl.pallas_call(functools.partial(exchange_kernel, tm_n, chan_n, early, 1....  199 us
    pallas_call x1, Pallas kernels, correlate_all(): pl.pallas_call(functools.partial(correlate_kernel, chan_n, channels, 1.0...  21.9 us

profile of v5, /device:TPU:1, one launch (start us, length us, event | category | flops | bytes accessed | tf_op | source)
XLA Modules:
  0.0 221.2 jit_solution(10585631004777453298)
XLA Ops:
  0.0 199.2 %shard_map.37 = (bf16[32,4,12,16,128]{4,3,2,1,0:T(8,128)(2,1)}, bf16[2,2,1024,1024]{3,2,1,0:T(8,128)(2,1)}) custom-call(bf16[128,68608]{1,0:T(8,128)(2,1)} %volt.1, f32[4,1024]{1,0:T(4,128)} %taper.1, bf16[512,1024]{1,0:T(8,128)(2,1)} %constant.2.clone.table_in), custom_call_target="tpu_custom_call" | custom-call | flops 8589934592 | bytes 41943040 | tf_op jit(solution)/shard_map/pallas_call | solution.py:241
  199.3 21.9 %shard_map.38 = bf16[8,2,1024,1024]{3,2,1,0:T(8,128)(2,1)} custom-call(bf16[32,4,12,16,128]{4,3,2,1,0:T(8,128)(2,1)} %get-tuple-element.7.spec, bf16[2,2,1024,1024]{3,2,1,0:T(8,128)(2,1)} %get-tuple-element.8.done), custom_call_target="tpu_custom_call" | custom-call | flops 12884901888 | bytes 31457280 | tf_op jit(solution)/shard_map/pallas_call | solution.py:337
